TPU v7x, 32 devices: a whole 2x2x4 slice. The times are simulated.
32 devices in a mesh: groups: 2 (over y), dom: 4 (over z), pole: 2 (over x), vec: 2 (over core).
Axes of the slice: x: 2, y: 2, z: 4, core: 2. Of those that a mesh axis runs over, the one named last changes fastest.
Arguments:
- right_side: bfloat16 [8192, 256], P(('groups', 'dom'), 'vec'), parts along dimension 0, may hold values from -8 to 8
- inverse: bfloat16 [2, 2, 8192, 1024], P('pole', None, ('groups', 'dom')), parts along dimension 2, may hold values from -2 to 2
- coupling: bfloat16 [8, 2, 256, 256], P(('groups', 'dom')), parts along dimension 0, may hold values from -1 to 1, as said below
- weights: float32 [2, 2], P('pole'), may hold values from -3 to 3
Outputs:
- basis: bfloat16 [8192, 256], P(('groups', 'dom'), 'vec'), parts along dimension 0
- factor: float32 [512, 256], P('groups'), parts along dimension 0
There are 2 independent parts, one for each index of `groups`. A program takes and returns all parts, laid end to end along the dimension named above; an argument that names none is the same for every part. Nothing has to cross between parts.
Inputs may be any that keep to these rules, and one draw needn't show every extreme that they name: coupling[d, 0] is the transpose of coupling[d - 1, 1]; coupling[0, 0] and coupling[3, 1] are zero.
All inputs are finite; a program needn't handle non-finite values.
Results may differ from a plain program's by a relative error of at most 0.0052.
Values may be sent and summed in bfloat16 or wider, within the bound.
A program may use at most 64 MiB of HBM per device.

v0:
```python
import jax
import jax.numpy as jnp
from jax import lax
from jax.sharding import PartitionSpec as P

SWEEPS = 2


def padded_2(block, sides, width):
    for axis, dim in sides:
        count = lax.axis_size(axis)
        forward = [(i, i + 1) for i in range(count - 1)]
        backward = [(target, source) for source, target in forward]
        low = lax.ppermute(
            lax.slice_in_dim(block, block.shape[dim] - width, None, axis=dim), axis, forward
        )
        high = lax.ppermute(lax.slice_in_dim(block, 0, width, axis=dim), axis, backward)
        block = jnp.concatenate([low, block, high], axis=dim)
    return block


def triangular(filtered, gram_sum, rows_total):
    factor = jnp.linalg.cholesky(gram_sum / rows_total)
    solved = lax.linalg.triangular_solve(
        factor, filtered, left_side=False, lower=True, transpose_a=True
    )
    return (solved, factor)


def body(right_side, inverse, coupling, weights):
    rows, width = right_side.shape
    edge = coupling.shape[2]
    source = right_side.astype(jnp.float32)
    empty = jnp.zeros_like(source)
    inv_re = inverse[0, 0]
    inv_im = inverse[0, 1]
    real = jnp.dot(inv_re, right_side, preferred_element_type=jnp.float32)
    imag = jnp.dot(inv_im, right_side, preferred_element_type=jnp.float32)
    field = jnp.stack([real, imag]).astype(jnp.bfloat16)
    for sweep in range(SWEEPS):
        padded = padded_2(field, (("dom", 1),), edge)
        above = padded[:, :edge]
        below = padded[:, edge + rows :]
        top = jnp.einsum("ab,cbm->cam", coupling[0, 0], above, preferred_element_type=jnp.float32)
        bottom = jnp.einsum(
            "ab,cbm->cam", coupling[0, 1], below, preferred_element_type=jnp.float32
        )
        rhs = jnp.stack([source, empty])
        rhs = rhs.at[:, :edge].add(top).at[:, rows - edge :].add(bottom).astype(jnp.bfloat16)
        real = jnp.dot(inv_re, rhs[0], preferred_element_type=jnp.float32) - jnp.dot(
            inv_im, rhs[1], preferred_element_type=jnp.float32
        )
        imag = jnp.dot(inv_re, rhs[1], preferred_element_type=jnp.float32) + jnp.dot(
            inv_im, rhs[0], preferred_element_type=jnp.float32
        )
        field = jnp.stack([real, imag])
        if sweep < SWEEPS - 1:
            field = field.astype(jnp.bfloat16)
    term = weights[0, 0] * field[0] - weights[0, 1] * field[1]
    rows_total = rows * lax.axis_size("dom")
    column_start = lax.axis_index("vec") * width
    filtered = lax.psum(term, "pole")
    whole_cols = lax.all_gather(filtered, "vec", axis=1, tiled=True)
    local_gram = jnp.dot(whole_cols.T, whole_cols, precision=lax.Precision.HIGHEST)
    gram_sum = lax.psum(local_gram, "dom")
    solved, factor = triangular(whole_cols, gram_sum, rows_total)
    basis = lax.dynamic_slice_in_dim(solved, column_start, width, 1).astype(jnp.bfloat16)
    return (basis, factor)


def solution(mesh):
    return jax.shard_map(
        body,
        mesh=mesh,
        in_specs=(
            P(("groups", "dom"), "vec"),
            P("pole", None, ("groups", "dom"), None),
            P(("groups", "dom"), None, None, None),
            P("pole", None),
        ),
        out_specs=(P(("groups", "dom"), "vec"), P("groups", None)),
        check_vma=False,
    )
```

profile of v0, /device:TPU:1, one launch (start us, length us, event | category | flops | bytes accessed | tf_op | source)
XLA Modules:
  0.0 192.6 jit_solution(9019263882079773760)
XLA Ops:
  7.2 2.3 %fusion.62 = bf16[1,1024,128]{2,1,0:T(8,128)(2,1)S(1)} fusion(bf16[1024,128]{1,0:T(8,128)(2,1)} %param.12, bf16[1,2,1024,1024]{3,2,1,0:T(8,128)(2,1)} %param.13), kind=kOutput, calls=%fused_computation.37 | convolution fusion | flops 268566528 | bytes 2621440 | tf_op jit(solution)/shard_map/dot_general | solution.py:38
  9.6 2.3 %fusion.65 = bf16[1,1024,128]{2,1,0:T(8,128)(2,1)S(1)} fusion(bf16[1024,128]{1,0:T(8,128)(2,1)} %param.12, bf16[1,2,1024,1024]{3,2,1,0:T(8,128)(2,1)} %param.13), kind=kOutput, calls=%fused_computation.38 | convolution fusion | flops 268566528 | bytes 2621440 | tf_op jit(solution)/shard_map/dot_general | solution.py:37
  11.9 4.0 %collective-permute-start = (bf16[2,256,128]{2,1,0:T(8,128)(2,1)S(1)}, bf16[2,256,128]{2,1,0:T(8,128)(2,1)S(1)}, u32[]{:S(2)}, u32[]{:S(2)}) collective-permute-start(bf16[2,256,128]{2,1,0:T(8,128)(2,1)S(1)} %get-tuple-element.75), channel_id=1, source_target_pairs={{0,4},{4,8},{8,12},{1,5},{5,9},{9,13},{2,6},{6,10},{10,14},{3,7},{... | collective-permute-start | bytes 393224 | tf_op jit(solution)/shard_map/ppermute | solution.py:14
  16.0 1.3 collective-permute-start.1
  18.4 3.3 %collective-permute-done.1 = bf16[2,256,128]{2,1,0:T(8,128)(2,1)S(1)} collective-permute-done((bf16[2,256,128]{2,1,0:T(8,128)(2,1)S(1)}, bf16[2,256,128]{2,1,0:T(8,128)(2,1)S(1)}, u32[]{:S(2)}, u32[]{:S(2)}) %collective-permute-start.1) | collective-permute-done | bytes 131104 | tf_op jit(solution)/shard_map/ppermute | solution.py:17
  25.4 3.2 %collective-permute-start.2 = (bf16[2,256,128]{1,2,0:T(8,128)(2,1)S(1)}, bf16[2,256,128]{1,2,0:T(8,128)(2,1)S(1)}, u32[]{:S(2)}, u32[]{:S(2)}) collective-permute-start(bf16[2,256,128]{1,2,0:T(8,128)(2,1)S(1)} %get-tuple-element.73), channel_id=1, source_target_pairs={{0,4},{4,8},{8,12},{1,5},{5,9},{9,13},{2,6},{6,10},{10,14},{3,7},{... | collective-permute-start | bytes 393224 | tf_op jit(solution)/shard_map/ppermute | solution.py:14
  29.2 1.3 collective-permute-start.3
  30.8 4.1 %collective-permute-done.3 = bf16[2,256,128]{1,2,0:T(8,128)(2,1)S(1)} collective-permute-done((bf16[2,256,128]{1,2,0:T(8,128)(2,1)S(1)}, bf16[2,256,128]{1,2,0:T(8,128)(2,1)S(1)}, u32[]{:S(2)}, u32[]{:S(2)}) %collective-permute-start.3) | collective-permute-done | bytes 131104 | tf_op jit(solution)/shard_map/ppermute | solution.py:17
  36.9 1.5 fusion.41
  38.4 2.3 %fusion.35 = f32[1024,128]{0,1:T(8,128)} fusion(f32[128,1024]{1,0:T(8,128)S(1)} %fusion.41, f32[128,1024]{1,0:T(8,128)S(1)} %fusion.2, bf16[1,2,1024,1024]{3,2,1,0:T(8,128)(2,1)S(1)} %copy-done.1, f32[]{:T(128)} %bitcast, bf16[2,1024,128]{1,2,0:T(8,128)(2,1)S(1)} %convert_element_type.13), kind=kOutput, calls=%fused_computation.27 | convolution fusion | flops 268828672 | bytes 3932164 | tf_op jit(solution)/shard_map/dot_general | solution.py:50
  40.8 30.8 %all-reduce.5.cloned.1.call-done = f32[1024,128]{0,1:T(8,128)} async-done(((f32[1024,128]{0,1:T(8,128)}), f32[1024,128]{0,1:T(8,128)}) %all-reduce.5.cloned.1.call-update) | async-done | bytes 524304 | tf_op jit(solution)/shard_map/psum | solution.py:62
  71.8 10.8 %all-gather.2.cloned.1.call-done = f32[1024,256]{0,1:T(8,128)} async-done(((f32[1024,128]{0,1:T(8,128)}), f32[1024,256]{0,1:T(8,128)}) %all-gather.2.cloned.1.call-update) | async-done | bytes 1048592 | tf_op jit(solution)/shard_map/all_gather | solution.py:63
  82.6 3.4 %fusion.109 = f32[256,256]{0,1:T(8,128)} fusion(f32[1024,256]{0,1:T(8,128)} %all-gather.2.cloned.1.call-done), kind=kOutput, calls=%fused_computation.110 | convolution fusion | flops 805306368 | bytes 1310720 | tf_op jit(solution)/shard_map/dot_general | solution.py:64
  86.0 34.9 %all-reduce.7.cloned.1.call-done = f32[256,256]{0,1:T(8,128)} async-done(((f32[256,256]{0,1:T(8,128)}), f32[256,256]{0,1:T(8,128)}) %all-reduce.7.cloned.1.call-update) | async-done | bytes 262160 | tf_op jit(solution)/shard_map/psum | solution.py:65
  120.9 1.0 broadcast_multiply_fusion
  122.0 1.0 fusion.88
  123.0 11.7 %cholesky.50 = f32[128,128]{1,0:T(8,128)S(1)} custom-call(f32[128,128]{1,0:T(8,128)S(1)} %cholesky.118), custom_call_target="Cholesky" | custom-call | tf_op jit(solution)/shard_map/jit(cholesky)/cholesky | solution.py:23
  134.8 9.8 %custom-call.14 = f32[1,128,128]{1,2,0:T(8,128)S(1)} custom-call(f32[1,128,128]{2,1,0:T(8,128)S(1)} %get-tuple-element.79), custom_call_target="InvertDiagBlocksLowerTriangular" | custom-call | tf_op jit(solution)/shard_map/jit(cholesky)/cholesky | solution.py:23
  145.1 11.7 %cholesky.105 = f32[128,128]{1,0:T(8,128)S(1)} custom-call(f32[128,128]{1,0:T(8,128)S(1)} %convolution_subtract_fusion.1), custom_call_target="Cholesky" | custom-call | tf_op jit(solution)/shard_map/jit(cholesky)/cholesky | solution.py:23
  159.6 4.0 %while.5 = (s32[]{:T(128)}, f32[256,256]{1,0:T(8,128)S(1)}, s32[2,2]{1,0:T(2,128)S(1)}, f32[2,128,128]{2,1,0:T(8,128)S(1)}, s32[]{:T(128)}) while((s32[]{:T(128)}, f32[256,256]{1,0:T(8,128)S(1)}, s32[2,2]{1,0:T(2,128)S(1)}, f32[2,128,128]{2,1,0:T(8,128)S(1)}, s32[]{:T(128)}) %tuple.48), condition=%wide.while_cond.4, body=%wide.while_body.4.sunk | while | flops 2 | bytes 131181 | solution.py:24
  160.2 1.4 bitcast_dynamic-update-slice_fusion.2
  162.2 1.4 bitcast_dynamic-update-slice_fusion.2
  163.6 19.7 %custom-call.15 = f32[2,128,128]{1,2,0:T(8,128)S(1)} custom-call(f32[2,128,128]{2,1,0:T(8,128)S(1)} %get-tuple-element.57), custom_call_target="InvertDiagBlocksLowerTriangular" | custom-call | tf_op jit(solution)/shard_map/triangular_solve | solution.py:24
  185.3 0.8 copy.11
  (56 shorter events, 13.2 us)
Async XLA Ops:
  7.2 10.1 %copy-start.3 = (bf16[1024,128]{1,0:T(8,128)(2,1)S(1)}, bf16[1024,128]{1,0:T(8,128)(2,1)}, u32[]{:S(2)}) copy-start(bf16[1024,128]{1,0:T(8,128)(2,1)} %param.12) | copy-start | bytes 786436
  7.2 64.4 %all-reduce.5.cloned.1.call-start = ((), (), s32[]{:S(2)}) async-start(), calls=%async_computation | async-start | bytes 1048576 | tf_op jit(solution)/shard_map/psum | solution.py:62
  9.6 8.6 %copy-start.2 = (bf16[1,2,256,256]{3,2,1,0:T(8,128)(2,1)S(1)}, bf16[1,2,256,256]{3,2,1,0:T(8,128)(2,1)}, u32[]{:S(2)}) copy-start(bf16[1,2,256,256]{3,2,1,0:T(8,128)(2,1)} %param.14) | copy-start | bytes 786436
  11.9 6.2 %collective-permute-start = (bf16[2,256,128]{2,1,0:T(8,128)(2,1)S(1)}, bf16[2,256,128]{2,1,0:T(8,128)(2,1)S(1)}, u32[]{:S(2)}, u32[]{:S(2)}) collective-permute-start(bf16[2,256,128]{2,1,0:T(8,128)(2,1)S(1)} %get-tuple-element.75), channel_id=1, source_target_pairs={{0,4},{4,8},{8,12},{1,5},{5,9},{9,13},{2,6},{6,10},{10,14},{3,7},{... | collective-permute-start | bytes 393224 | tf_op jit(solution)/shard_map/ppermute | solution.py:14
  16.0 5.7 %collective-permute-start.1 = (bf16[2,256,128]{2,1,0:T(8,128)(2,1)S(1)}, bf16[2,256,128]{2,1,0:T(8,128)(2,1)S(1)}, u32[]{:S(2)}, u32[]{:S(2)}) collective-permute-start(bf16[2,256,128]{2,1,0:T(8,128)(2,1)S(1)} %get-tuple-element.74), channel_id=1, source_target_pairs={{4,0},{8,4},{12,8},{5,1},{9,5},{13,9},{6,2},{10,6},{14,10},{7,3},{... | collective-permute-start | bytes 393224 | tf_op jit(solution)/shard_map/ppermute | solution.py:17
  17.4 4.6 %copy-start.1 = (bf16[1,2,1024,1024]{3,2,1,0:T(8,128)(2,1)S(1)}, bf16[1,2,1024,1024]{3,2,1,0:T(8,128)(2,1)}, u32[]{:S(2)}) copy-start(bf16[1,2,1024,1024]{3,2,1,0:T(8,128)(2,1)} %param.13) | copy-start | bytes 12582916
  23.7 4.9 %copy-start.4 = (f32[1,2]{1,0:T(1,128)S(1)}, f32[1,2]{1,0:T(1,128)}, u32[]{:S(2)}) copy-start(f32[1,2]{1,0:T(1,128)} %param.15) | copy-start | bytes 28
  25.4 5.1 %collective-permute-start.2 = (bf16[2,256,128]{1,2,0:T(8,128)(2,1)S(1)}, bf16[2,256,128]{1,2,0:T(8,128)(2,1)S(1)}, u32[]{:S(2)}, u32[]{:S(2)}) collective-permute-start(bf16[2,256,128]{1,2,0:T(8,128)(2,1)S(1)} %get-tuple-element.73), channel_id=1, source_target_pairs={{0,4},{4,8},{8,12},{1,5},{5,9},{9,13},{2,6},{6,10},{10,14},{3,7},{... | collective-permute-start | bytes 393224 | tf_op jit(solution)/shard_map/ppermute | solution.py:14
  29.2 5.7 %collective-permute-start.3 = (bf16[2,256,128]{1,2,0:T(8,128)(2,1)S(1)}, bf16[2,256,128]{1,2,0:T(8,128)(2,1)S(1)}, u32[]{:S(2)}, u32[]{:S(2)}) collective-permute-start(bf16[2,256,128]{1,2,0:T(8,128)(2,1)S(1)} %get-tuple-element.72), channel_id=1, source_target_pairs={{4,0},{8,4},{12,8},{5,1},{9,5},{13,9},{6,2},{10,6},{14,10},{7,3},{... | collective-permute-start | bytes 393224 | tf_op jit(solution)/shard_map/ppermute | solution.py:17
  40.7 41.9 %all-gather.2.cloned.1.call-start = ((), (), s32[]{:S(2)}) async-start(), calls=%async_computation.1 | async-start | bytes 1572864 | tf_op jit(solution)/shard_map/all_gather | solution.py:63
  71.6 49.4 %all-reduce.7.cloned.1.call-start = ((), (), s32[]{:S(2)}) async-start(), calls=%async_computation.2 | async-start | bytes 524288 | tf_op jit(solution)/shard_map/psum | solution.py:65
  82.6 100.7 %copy-start = (f32[1024,256]{0,1:T(8,128)S(1)}, f32[1024,256]{0,1:T(8,128)}, u32[]{:S(2)}) copy-start(f32[1024,256]{0,1:T(8,128)} %all-gather.2.cloned.1.call-done) | copy-start | bytes 3145732
Sparse Core Ops, SparseCore 0:
  40.8 30.6 all-reduce.4
  73.1 9.4 all-gather.1
  86.1 34.7 all-reduce.6
where the time goes:
time: 195 us; the launch traced here: 193 us
  waiting for transfers between devices  84.5 us (43%)
  other arithmetic  56.7 us (29%)
  matrix products  20 us (10%)
  between operations  15.4 us (8%)
  starting transfers between devices  10.1 us (5%)
  local copies, waits for them, and re-layouts  5.82 us (3%)
    psum x1, waiting for transfers between devices, body(): gram_sum = lax.psum(local_gram, 'dom')  34.9 us
    another operation x6, other arithmetic, triangular(): factor = jnp.linalg.cholesky(gram_sum / rows_total)  33.9 us
    psum x1, waiting for transfers between devices, body(): filtered = lax.psum(term, 'pole')  30.8 us
    another operation x3, other arithmetic, triangular(): lax.linalg.triangular_solve(factor, filtered, left_side=False, lower=True...  20.4 us
    all_gather x1, waiting for transfers between devices, body(): whole_cols = lax.all_gather(filtered, 'vec', axis=1, tiled=True)  10.8 us
    ppermute x2, waiting for transfers between devices, padded_2(): lax.ppermute(lax.slice_in_dim(block, 0, width, axis=dim), axis, backward)  7.46 us
    ppermute x2, starting transfers between devices, padded_2(): lax.ppermute(lax.slice_in_dim(block, block.shape[dim] - width, None, axis...  7.24 us
    another operation x6, local copies, waits for them, and re-layouts  3.93 us
  transfers between devices with their start and end apart: 7, of which 6 were waited for; matrix products, arithmetic and copies ran while one was open for 1% of the time, Pallas kernels for 0%

commit v1 on v0

v1 whole, which is shorter than its diff:
```python
import functools

import jax
import jax.numpy as jnp
from jax import lax
from jax.experimental import pallas as pl
from jax.experimental.pallas import tpu as pltpu
from jax.sharding import PartitionSpec as P

MESH = pl.DeviceIdType.MESH
HI = lax.Precision.HIGHEST
F32 = jnp.float32
BF16 = jnp.bfloat16
CHUNKS = 4


def mm(a, b):
    return jnp.dot(a, b, preferred_element_type=F32)


def tmm(a, b):
    return lax.dot_general(
        a, b, (((0,), (0,)), ((), ())), precision=HI, preferred_element_type=F32
    )


def hmm(a, b):
    return jnp.dot(a, b, precision=HI, preferred_element_type=F32)


def filter_kernel(
    nd, np_, x_ref, inv_ref, k_ref, w_ref, q_ref, g_ref,
    y0, edges, ends, pbuf, dbuf, gpart, gslot,
    e_send, e_recv, p_send, p_recv, d_send, d_recv, v_send, v_recv,
    r_send, r_recv, a_send, a_recv, f_send, f_recv,
):
    d = lax.axis_index("dom")
    p = lax.axis_index("pole")
    v = lax.axis_index("vec")
    rows, width = x_ref.shape
    edge = k_ref.shape[2]
    tall = rows // CHUNKS
    piece = g_ref.shape[1] // nd
    a_ref, c_ref = inv_ref.at[0, 0], inv_ref.at[0, 1]
    has_low, has_high = d > 0, d < nd - 1

    def dom(k):
        return {"dom": lax.rem(d + k, nd)}

    def pole(k):
        return {"pole": lax.rem(p + k, np_)}

    other = {"vec": 1 - v}

    barrier = pltpu.get_barrier_semaphore()
    for k in range(1, nd):
        pl.semaphore_signal(barrier, inc=1, device_id=dom(k), device_id_type=MESH)
    for k in range(1, np_):
        pl.semaphore_signal(barrier, inc=1, device_id=pole(k), device_id_type=MESH)
    pl.semaphore_signal(barrier, inc=1, device_id=other, device_id_type=MESH)

    @pl.when(jnp.logical_not(has_low))
    def _():
        ends[0, 0] = jnp.zeros(ends.shape[2:], BF16)
        ends[1, 0] = jnp.zeros(ends.shape[2:], BF16)

    @pl.when(jnp.logical_not(has_high))
    def _():
        ends[0, 1] = jnp.zeros(ends.shape[2:], BF16)
        ends[1, 1] = jnp.zeros(ends.shape[2:], BF16)

    pl.semaphore_wait(barrier, nd + np_ - 1)

    def copy(src, dst, send, recv, device):
        return pltpu.make_async_remote_copy(
            src_ref=src, dst_ref=dst, send_sem=send, recv_sem=recv,
            device_id=device, device_id_type=MESH,
        )

    def swap_ends(s):
        up = copy(edges.at[s, 1], ends.at[s, 0], e_send.at[s, 0], e_recv.at[s, 0], {"dom": d + 1})
        down = copy(edges.at[s, 0], ends.at[s, 1], e_send.at[s, 1], e_recv.at[s, 1], {"dom": d - 1})
        return up, down

    def start_ends(s):
        up, down = swap_ends(s)
        pl.when(has_high)(up.start)
        pl.when(has_low)(down.start)

    def wait_ends(s):
        up, down = swap_ends(s)
        pl.when(has_low)(up.wait_recv)
        pl.when(has_high)(down.wait_recv)
        pl.when(has_high)(up.wait_send)
        pl.when(has_low)(down.wait_send)

    x = x_ref[...]

    def first(lo):
        y0[lo : lo + edge, :width] = mm(a_ref[lo : lo + edge, :], x)
        y0[lo : lo + edge, width:] = mm(c_ref[lo : lo + edge, :], x)

    last = rows - edge
    for n, lo in enumerate((0, last)):
        first(lo)
        edges[0, n] = y0[lo : lo + edge, :].astype(BF16)
    start_ends(0)

    for lo in range(edge, last, edge):
        first(lo)
    w0, w1 = w_ref[0, 0], w_ref[0, 1]

    def source_part(lo, count):
        return w0 * y0[lo : lo + count, :width] - w1 * y0[lo : lo + count, width:]

    for lo in range(0, rows, tall):
        pbuf[p, lo : lo + tall] = source_part(lo, tall).astype(BF16)
    p_copies = [
        copy(pbuf.at[p], pbuf.at[p], p_send.at[k], p_recv.at[k], pole(k)) for k in range(1, np_)
    ]
    for c in p_copies:
        c.start()

    wait_ends(0)

    def turned(u):
        return jnp.concatenate([-u[:, width:], u[:, :width]], axis=1)

    tops = [mm(k_ref[0, n], ends[0, n]) for n in range(2)]
    plain = [t.astype(BF16) for t in tops]
    swapped = [turned(t).astype(BF16) for t in tops]
    for n, lo in enumerate((0, last)):
        total = y0[lo : lo + edge, :]
        for m, col in enumerate((0, last)):
            total += mm(a_ref[lo : lo + edge, col : col + edge], plain[m])
            total += mm(c_ref[lo : lo + edge, col : col + edge], swapped[m])
        edges[1, n] = total.astype(BF16)
    start_ends(1)
    wait_ends(1)

    tops = [mm(k_ref[0, n], ends[1, n]) for n in range(2)]
    gs = [(w0 * t[:, :width] - w1 * t[:, width:]).astype(BF16) for t in tops]
    hs = [(-w0 * t[:, width:] - w1 * t[:, :width]).astype(BF16) for t in tops]
    d_copies = []
    for i in range(CHUNKS):
        lo = i * tall
        part = source_part(lo, tall)
        total = part - part.astype(BF16).astype(F32)
        for m, col in enumerate((0, last)):
            total += mm(a_ref[lo : lo + tall, col : col + edge], gs[m])
            total += mm(c_ref[lo : lo + tall, col : col + edge], hs[m])
        dbuf[p, lo : lo + tall] = total.astype(BF16)
        here = dbuf.at[p, lo : lo + tall]
        d_copies.append([
            copy(here, here, d_send.at[i, k], d_recv.at[i, k], pole(k)) for k in range(1, np_)
        ])
        for c in d_copies[-1]:
            c.start()

    for c in p_copies:
        c.wait()
    v_copies = []
    for i in range(CHUNKS):
        lo = i * tall
        for c in d_copies[i]:
            c.wait()
        total = jnp.zeros((tall, width), F32)
        for q in range(np_):
            total += pbuf[q, lo : lo + tall].astype(F32) + dbuf[q, lo : lo + tall].astype(F32)
        q_ref[v, lo : lo + tall] = total
        here = q_ref.at[v, lo : lo + tall]
        v_copies.append(copy(here, here, v_send.at[i], v_recv.at[i], other))
        v_copies[-1].start()

    sums = [jnp.zeros((width, width), F32) for _ in range(2)]
    for i in range(CHUNKS):
        lo = i * tall
        v_copies[i].wait()
        mine = q_ref[v, lo : lo + tall]
        for u in range(2):
            sums[u] += tmm(q_ref[u, lo : lo + tall], mine)
    for u in range(2):
        gpart[u * width : (u + 1) * width] = sums[u]

    def own(k):
        return pl.ds(pl.multiple_of(lax.rem(d + k, nd) * piece, piece), piece)

    r_copies = [
        copy(gpart.at[own(k)], gslot.at[d], r_send.at[k], r_recv.at[k], dom(k))
        for k in range(1, nd)
    ]
    for c in r_copies:
        c.start()
    gslot[d] = gpart[own(0)]
    for c in r_copies:
        c.wait()
    total = gslot[0]
    for q in range(1, nd):
        total += gslot[q]
    g_ref[v, own(0)] = total
    here = g_ref.at[v, own(0)]
    a_copies = [copy(here, here, a_send.at[k], a_recv.at[k], dom(k)) for k in range(1, nd)]
    for c in a_copies:
        c.start()
    f_copies = []
    for k in range(nd):
        if k > 0:
            a_copies[k - 1].wait_recv()
        here = g_ref.at[v, own(nd - k)]
        f_copies.append(copy(here, here, f_send.at[k], f_recv.at[k], other))
        f_copies[-1].start()
    for c in a_copies:
        c.wait_send()
    for c in f_copies:
        c.wait()


def eliminate(w):
    n = w.shape[0]
    sub = lax.broadcasted_iota(jnp.int32, (8, n), 0)
    lane = lax.broadcasted_iota(jnp.int32, (8, n), 1)
    groups = n // 8
    ws = [w[8 * g : 8 * g + 8] for g in range(groups)]
    es = [(lane == sub + 8 * g).astype(F32) for g in range(groups)]
    upper, lower = [], []
    for b in range(groups):
        k = 8 * b
        pw, pe = ws[b], es[b]
        cols = [jnp.broadcast_to(pw[:, k + j : k + j + 1], (8, n)) for j in range(8)]
        far = [
            [jnp.broadcast_to(ws[g][:, k + j : k + j + 1], (8, n)) for j in range(8)]
            for g in range(b + 1, groups)
        ]
        uw, ue = jnp.zeros_like(pw), jnp.zeros_like(pe)
        for j in range(8):
            at = sub == j
            c = cols[j]
            pivot = c[j : j + 1]
            root = lax.rsqrt(pivot)
            inverse = 1.0 / pivot
            rw, re = pw[j : j + 1], pe[j : j + 1]
            uw = jnp.where(at, rw * root, uw)
            ue = jnp.where(at, re * root, ue)
            rw, re = rw * inverse, re * inverse
            pw = jnp.where(at, rw, pw - c * rw)
            pe = jnp.where(at, re, pe - c * re)
            for m in range(j + 1, 8):
                rc = cols[m][j : j + 1] * inverse
                cols[m] = jnp.where(at, rc, cols[m] - c * rc)
        upper.append(uw)
        lower.append(ue)
        for g in range(b + 1, groups):
            for j in range(8):
                c = far[g - b - 1][j]
                ws[g] = ws[g] - c * pw[j : j + 1]
                es[g] = es[g] - c * pe[j : j + 1]
    u = jnp.concatenate(upper, axis=0)
    l = jnp.concatenate(lower, axis=0)
    row = lax.broadcasted_iota(jnp.int32, (n, n), 0)
    col = lax.broadcasted_iota(jnp.int32, (n, n), 1)
    return jnp.where(row <= col, u, 0.0), jnp.where(row >= col, l, 0.0)


def solve_kernel(rows_total, q_ref, g_ref, basis_ref, factor_ref):
    v = lax.axis_index("vec")
    width = g_ref.shape[2]
    scale = 1.0 / rows_total
    u11, i11 = eliminate(g_ref[0, :width] * scale)
    u12 = hmm(i11, g_ref[1, :width] * scale)
    schur = g_ref[1, width:] * scale - tmm(u12, u12)
    u22, i22 = eliminate(schur)
    factor_ref[:width, :width] = u11.T
    factor_ref[:width, width:] = jnp.zeros((width, width), F32)
    factor_ref[width:, :width] = u12.T
    factor_ref[width:, width:] = u22.T

    def times(a, b):
        return lax.dot_general(
            a, b, (((1,), (1,)), ((), ())), precision=HI, preferred_element_type=F32
        )

    @pl.when(v == 0)
    def _():
        basis_ref[...] = times(q_ref[0], i11).astype(BF16)

    @pl.when(v == 1)
    def _():
        i21 = -hmm(i22, tmm(u12, i11))
        basis_ref[...] = (times(q_ref[0], i21) + times(q_ref[1], i22)).astype(BF16)


def body(right_side, inverse, coupling, weights):
    rows, width = right_side.shape
    edge = coupling.shape[2]
    nd, np_ = lax.axis_size("dom"), lax.axis_size("pole")
    vmem = pl.BlockSpec(memory_space=pltpu.VMEM)
    smem = pl.BlockSpec(memory_space=pltpu.SMEM)
    dma = pltpu.SemaphoreType.DMA
    q, g = pl.pallas_call(
        functools.partial(filter_kernel, nd, np_),
        out_shape=(
            jax.ShapeDtypeStruct((2, rows, width), F32),
            jax.ShapeDtypeStruct((2, 2 * width, width), F32),
        ),
        in_specs=[vmem, vmem, vmem, smem],
        out_specs=(vmem, vmem),
        scratch_shapes=[
            pltpu.VMEM((rows, 2 * width), F32),
            pltpu.VMEM((2, 2, edge, 2 * width), BF16),
            pltpu.VMEM((2, 2, edge, 2 * width), BF16),
            pltpu.VMEM((np_, rows, width), BF16),
            pltpu.VMEM((np_, rows, width), BF16),
            pltpu.VMEM((2 * width, width), F32),
            pltpu.VMEM((nd, 2 * width // nd, width), F32),
            dma((2, 2)), dma((2, 2)),
            dma((np_,)), dma((np_,)),
            dma((CHUNKS, np_)), dma((CHUNKS, np_)),
            dma((CHUNKS,)), dma((CHUNKS,)),
            dma((nd,)), dma((nd,)),
            dma((nd,)), dma((nd,)),
            dma((nd,)), dma((nd,)),
        ],
        compiler_params=pltpu.CompilerParams(
            collective_id=0, has_side_effects=True, vmem_limit_bytes=40 * 2**20
        ),
        name="filter",
    )(right_side, inverse, coupling, weights)
    return pl.pallas_call(
        functools.partial(solve_kernel, rows * nd),
        out_shape=(
            jax.ShapeDtypeStruct((rows, width), BF16),
            jax.ShapeDtypeStruct((2 * width, 2 * width), F32),
        ),
        in_specs=[vmem, vmem],
        out_specs=(vmem, vmem),
        compiler_params=pltpu.CompilerParams(vmem_limit_bytes=40 * 2**20),
        name="solve",
    )(q, g)


def solution(mesh):
    return jax.shard_map(
        body,
        mesh=mesh,
        in_specs=(
            P(("groups", "dom"), "vec"),
            P("pole", None, ("groups", "dom"), None),
            P(("groups", "dom"), None, None, None),
            P("pole", None),
        ),
        out_specs=(P(("groups", "dom"), "vec"), P("groups", None)),
        check_vma=False,
    )
```

time: 195 us -> 50 us (0.26); the launches traced: 193 us -> 49.8 us
  waiting for transfers between devices: 84.5 us -> 0 us
  other arithmetic: 56.7 us -> 0 us
  Pallas kernels: 0 us -> 44.4 us
  matrix products: 20 us -> 0 us
  between operations: 15.4 us -> 0.65 us
  starting transfers between devices: 10.1 us -> 0 us
    psum x2 -> x0, waiting for transfers between devices: 65.7 us -> none  [the longest x1 34.9 us: body(): gram_sum = lax.psum(local_gram, 'dom')]
    another operation x12 -> x0, other arithmetic: 54.5 us -> none  [the longest x6 33.9 us: triangular(): factor = jnp.linalg.cholesky(gram_sum / rows_total)]
    pallas_call x0 -> x2, Pallas kernels: none -> 44.4 us  [the longest x1 34 us: body(): pl.pallas_call(functools.partial(filter_kernel, nd, np_), out_shape=(jax....]
    dot_general x15 -> x0, matrix products: 17.7 us -> none  [the longest x1 3.36 us: body(): jnp.dot(whole_cols.T, whole_cols, precision=lax.Precision.HIGHEST)]
    all_gather x1 -> x0, waiting for transfers between devices: 10.8 us -> none  [body(): whole_cols = lax.all_gather(filtered, 'vec', axis=1, tiled=True)]
    ppermute x4 -> x0, starting transfers between devices: 9.81 us -> none  [the longest x2 7.24 us: padded_2(): lax.ppermute(lax.slice_in_dim(block, block.shape[dim] - width, None, axis...]
    ppermute x4 -> x0, waiting for transfers between devices: 7.98 us -> none  [the longest x2 7.46 us: padded_2(): lax.ppermute(lax.slice_in_dim(block, 0, width, axis=dim), axis, backward)]
    another operation x9 -> x0, local copies, waits for them, and re-layouts: 4.02 us -> none
  transfers between devices with their start and end apart: 7 -> 0, of which waited for: 6 -> 0; matrix products, arithmetic and copies ran while one was open for 1% -> 0% of each run, Pallas kernels for 0% -> 0%
where the time goes in v1:
time: 50 us; the launch traced here: 49.8 us
  Pallas kernels  44.4 us (89%)
  local copies, waits for them, and re-layouts  4.73 us (9%)
  between operations  0.65 us (1%)
    pallas_call x1, Pallas kernels, body(): pl.pallas_call(functools.partial(filter_kernel, nd, np_), out_shape=(jax....  34 us
    pallas_call x1, Pallas kernels, body(): pl.pallas_call(functools.partial(solve_kernel, rows * nd), out_shape=(jax...  10.4 us
    unnamed x8, local copies, waits for them, and re-layouts  4.73 us

profile of v1, /device:TPU:1, one launch (start us, length us, event | category | flops | bytes accessed | tf_op | source)
XLA Modules:
  0.0 49.8 jit_solution(12546667727342778682)
XLA Ops:
  0.6 0.0 copy-start
  0.6 2.2 %copy-done = bf16[1,2,1024,1024]{3,2,1,0:T(8,128)(2,1)S(1)} copy-done((bf16[1,2,1024,1024]{3,2,1,0:T(8,128)(2,1)S(1)}, bf16[1,2,1024,1024]{3,2,1,0:T(8,128)(2,1)}, u32[]{:S(2)}) %copy-start) | copy-done | bytes 4194328
  2.8 0.0 copy-start.1
  2.8 0.9 %copy-done.1 = bf16[1024,128]{1,0:T(8,128)(2,1)S(1)} copy-done((bf16[1024,128]{1,0:T(8,128)(2,1)S(1)}, bf16[1024,128]{1,0:T(8,128)(2,1)}, u32[]{:S(2)}) %copy-start.1) | copy-done | bytes 262168
  3.8 0.0 copy-start.2
  3.8 0.9 %copy-done.2 = bf16[1,2,256,256]{3,2,1,0:T(8,128)(2,1)S(1)} copy-done((bf16[1,2,256,256]{3,2,1,0:T(8,128)(2,1)S(1)}, bf16[1,2,256,256]{3,2,1,0:T(8,128)(2,1)}, u32[]{:S(2)}) %copy-start.2) | copy-done | bytes 262168
  4.7 0.0 copy-start.3
  4.7 0.7 %copy-done.3 = f32[1,2]{1,0:T(1,128)S(1)} copy-done((f32[1,2]{1,0:T(1,128)S(1)}, f32[1,2]{1,0:T(1,128)}, u32[]{:S(2)}) %copy-start.3) | copy-done | bytes 32
  5.4 34.0 %filter.1 = (f32[2,1024,128]{2,1,0:T(8,128)S(1)}, f32[2,256,128]{2,1,0:T(8,128)S(1)}) custom-call(bf16[1024,128]{1,0:T(8,128)(2,1)S(1)} %copy-done.1, bf16[1,2,1024,1024]{3,2,1,0:T(8,128)(2,1)S(1)} %copy-done, bf16[1,2,256,256]{3,2,1,0:T(8,128)(2,1)S(1)} %copy-done.2, f32[1,2]{1,0:T(1,128)S(1)} %copy-done.3), custom_call_target="tpu_custom_call" | custom-call | tf_op jit(solution)/shard_map/filter/pallas_call | solution.py:299
  39.4 10.4 %solve.1 = (bf16[1024,128]{1,0:T(8,128)(2,1)}, f32[256,256]{1,0:T(8,128)}) custom-call(f32[2,1024,128]{2,1,0:T(8,128)S(1)} %get-tuple-element.4.q_ref, f32[2,256,128]{2,1,0:T(8,128)S(1)} %get-tuple-element.5.g_ref), custom_call_target="tpu_custom_call" | custom-call | tf_op jit(solution)/shard_map/solve/pallas_call | solution.py:328
Async XLA Ops:
  0.6 2.2 %copy-start = (bf16[1,2,1024,1024]{3,2,1,0:T(8,128)(2,1)S(1)}, bf16[1,2,1024,1024]{3,2,1,0:T(8,128)(2,1)}, u32[]{:S(2)}) copy-start(bf16[1,2,1024,1024]{3,2,1,0:T(8,128)(2,1)} %inv_ref.1) | copy-start | bytes 12582916
  2.8 0.9 %copy-start.1 = (bf16[1024,128]{1,0:T(8,128)(2,1)S(1)}, bf16[1024,128]{1,0:T(8,128)(2,1)}, u32[]{:S(2)}) copy-start(bf16[1024,128]{1,0:T(8,128)(2,1)} %x_ref.1) | copy-start | bytes 786436
  3.8 0.9 %copy-start.2 = (bf16[1,2,256,256]{3,2,1,0:T(8,128)(2,1)S(1)}, bf16[1,2,256,256]{3,2,1,0:T(8,128)(2,1)}, u32[]{:S(2)}) copy-start(bf16[1,2,256,256]{3,2,1,0:T(8,128)(2,1)} %k_ref.1) | copy-start | bytes 786436
  4.7 0.7 %copy-start.3 = (f32[1,2]{1,0:T(1,128)S(1)}, f32[1,2]{1,0:T(1,128)}, u32[]{:S(2)}) copy-start(f32[1,2]{1,0:T(1,128)} %w_ref.1) | copy-start | bytes 28

commit v2 on v1

v2 whole, which is shorter than its diff:
```python
import functools

import jax
import jax.numpy as jnp
from jax import lax
from jax.experimental import pallas as pl
from jax.experimental.pallas import tpu as pltpu
from jax.sharding import PartitionSpec as P

MESH = pl.DeviceIdType.MESH
HI = lax.Precision.HIGHEST
F32 = jnp.float32
BF16 = jnp.bfloat16
CHUNKS = 2


def mm(a, b):
    return jnp.dot(a, b, preferred_element_type=F32)


def tmm(a, b):
    return lax.dot_general(
        a, b, (((0,), (0,)), ((), ())), precision=HI, preferred_element_type=F32
    )


def hmm(a, b):
    return jnp.dot(a, b, precision=HI, preferred_element_type=F32)


def times(a, b):
    return lax.dot_general(
        a, b, (((1,), (1,)), ((), ())), precision=HI, preferred_element_type=F32
    )


def repeat(lo, hi, step):
    if hi - lo <= 16:
        for k in range(lo, hi):
            step(k)
    else:
        lax.fori_loop(lo, hi, lambda k, _: (step(k), 0)[1], 0)


def piece_of(total, owners):
    piece = 8
    while total % piece or total // piece > owners:
        piece += 8
    return piece


def filter_kernel(
    nd, np_, x_hbm, inv_hbm, k_hbm, w_hbm, q_ref, g_ref,
    x_ref, inv_ref, k_ref, w_ref, l_sem, y0, edges, ends, psend, pslot, dsend, dslot,
    cross, gpart, gslot,
    e_send, e_recv, p_send, p_recv, d_send, d_recv, v_send, v_recv,
    q_send, q_recv, h_send, h_recv, r_send, r_recv, a_send, a_recv, f_send, f_recv,
):
    d = lax.axis_index("dom")
    p = lax.axis_index("pole")
    v = lax.axis_index("vec")
    rows, width = x_ref.shape
    edge = k_ref.shape[1]
    last = rows - edge
    share = rows // np_
    tall = share // CHUNKS
    half = width // 2
    owners = nd * np_
    piece = gslot.shape[1]
    pieces = g_ref.shape[1] // piece
    me = d * np_ + p
    a_ref, c_ref = inv_ref.at[0], inv_ref.at[1]
    has_low, has_high = d > 0, d < nd - 1
    other = {"vec": 1 - v}

    def at(k):
        return lax.rem(me + k, owners)

    def device(o):
        return {"dom": lax.div(o, np_), "pole": lax.rem(o, np_)}

    def pole(k):
        return lax.rem(p + k, np_)

    def when_owner(o, act):
        if pieces == owners:
            act()
        else:
            pl.when(o < pieces)(act)

    loads = [pltpu.make_async_copy(x_hbm, x_ref, l_sem.at[0])]
    for n, (lo, count) in enumerate(((0, edge), (last, edge), (edge, last - edge))):
        loads.append(
            pltpu.make_async_copy(
                inv_hbm.at[0, :, lo : lo + count], inv_ref.at[:, lo : lo + count], l_sem.at[n + 1]
            )
        )
    loads.append(pltpu.make_async_copy(k_hbm.at[0], k_ref, l_sem.at[4]))
    loads.append(pltpu.make_async_copy(w_hbm, w_ref, l_sem.at[5]))
    for c in loads:
        c.start()

    barrier = pltpu.get_barrier_semaphore()

    def greet(k):
        pl.semaphore_signal(barrier, inc=1, device_id=device(at(k)), device_id_type=MESH)

    repeat(1, owners, greet)
    pl.semaphore_signal(barrier, inc=1, device_id=other, device_id_type=MESH)

    @pl.when(jnp.logical_not(has_low))
    def _():
        ends[0, 0] = jnp.zeros(ends.shape[2:], BF16)
        ends[1, 0] = jnp.zeros(ends.shape[2:], BF16)

    @pl.when(jnp.logical_not(has_high))
    def _():
        ends[0, 1] = jnp.zeros(ends.shape[2:], BF16)
        ends[1, 1] = jnp.zeros(ends.shape[2:], BF16)

    def copy(src, dst, send, recv, target):
        return pltpu.make_async_remote_copy(
            src_ref=src, dst_ref=dst, send_sem=send, recv_sem=recv,
            device_id=target, device_id_type=MESH,
        )

    def swap_ends(s):
        down = copy(edges.at[s, 0], ends.at[s, 1], e_send.at[s, 1], e_recv.at[s, 1], {"dom": d - 1})
        up = copy(edges.at[s, 1], ends.at[s, 0], e_send.at[s, 0], e_recv.at[s, 0], {"dom": d + 1})
        return down, up

    def start_end(s, n):
        pl.when((has_low, has_high)[n])(swap_ends(s)[n].start)

    def wait_ends(s):
        down, up = swap_ends(s)
        pl.when(has_low)(up.wait_recv)
        pl.when(has_high)(down.wait_recv)
        pl.when(has_high)(up.wait_send)
        pl.when(has_low)(down.wait_send)

    loads[0].wait()
    x = x_ref[...]

    def first(lo):
        y0[lo : lo + edge, :width] = mm(a_ref[lo : lo + edge, :], x)
        y0[lo : lo + edge, width:] = mm(c_ref[lo : lo + edge, :], x)

    for n, lo in enumerate((0, last)):
        loads[n + 1].wait()
        first(lo)
        edges[0, n] = y0[lo : lo + edge, :].astype(BF16)
        if n == 0:
            pl.semaphore_wait(barrier, owners)
        start_end(0, n)

    for c in loads[3:]:
        c.wait()
    for lo in range(edge, last, edge):
        first(lo)
    w0, w1 = w_ref[0, 0], w_ref[0, 1]

    def block(q, i):
        return pl.ds(pl.multiple_of(q * share + i * tall, tall), tall)

    def source_part(at_rows):
        return w0 * y0[at_rows, :width] - w1 * y0[at_rows, width:]

    p_copies = []
    for k in range(1, np_):
        q = pole(k)
        for i in range(CHUNKS):
            psend[k, i * tall : (i + 1) * tall] = source_part(block(q, i)).astype(BF16)
        p_copies.append(copy(psend.at[k], pslot.at[k], p_send.at[k], p_recv.at[k], {"pole": q}))
        p_copies[-1].start()

    wait_ends(0)

    def turned(u):
        return jnp.concatenate([-u[:, width:], u[:, :width]], axis=1)

    tops = [mm(k_ref[n], ends[0, n]) for n in range(2)]
    plain = [t.astype(BF16) for t in tops]
    swapped = [turned(t).astype(BF16) for t in tops]
    for n, lo in enumerate((0, last)):
        total = y0[lo : lo + edge, :]
        for m, col in enumerate((0, last)):
            total += mm(a_ref[lo : lo + edge, col : col + edge], plain[m])
            total += mm(c_ref[lo : lo + edge, col : col + edge], swapped[m])
        edges[1, n] = total.astype(BF16)
        start_end(1, n)
    wait_ends(1)

    tops = [mm(k_ref[n], ends[1, n]) for n in range(2)]
    gs = [(w0 * t[:, :width] - w1 * t[:, width:]).astype(BF16) for t in tops]
    hs = [(-w0 * t[:, width:] - w1 * t[:, :width]).astype(BF16) for t in tops]

    def correction(at_rows):
        total = jnp.zeros((tall, width), F32)
        for m, col in enumerate((0, last)):
            total += mm(a_ref[at_rows, col : col + edge], gs[m])
            total += mm(c_ref[at_rows, col : col + edge], hs[m])
        return total

    d_copies = [[] for _ in range(CHUNKS)]
    for i in range(CHUNKS):
        for k in range(1, np_):
            q = pole(k)
            part = source_part(block(q, i))
            part = part - part.astype(BF16).astype(F32) + correction(block(q, i))
            here = slice(i * tall, (i + 1) * tall)
            dsend[k, here] = part.astype(BF16)
            c = copy(
                dsend.at[k, here], dslot.at[k, here], d_send.at[i, k], d_recv.at[i, k], {"pole": q}
            )
            c.start()
            d_copies[i].append(c)
    for i in range(CHUNKS):
        q_ref[v, block(p, i)] = source_part(block(p, i)) + correction(block(p, i))

    for c in p_copies:
        c.wait()
    v_copies = []
    for i in range(CHUNKS):
        for c in d_copies[i]:
            c.wait()
        total = q_ref[v, block(p, i)]
        here = slice(i * tall, (i + 1) * tall)
        for k in range(1, np_):
            total += pslot[k, here].astype(F32) + dslot[k, here].astype(F32)
        q_ref[v, block(p, i)] = total
        mine = q_ref.at[v, block(p, i)]
        v_copies.append(copy(mine, mine, v_send.at[i], v_recv.at[i], other))
        v_copies[-1].start()

    diagonal = jnp.zeros((width, width), F32)
    below = jnp.zeros((width, width), F32)
    for i in range(CHUNKS):
        mine = q_ref[v, block(p, i)]
        diagonal += tmm(mine, mine)
    gpart[:width] = diagonal
    for i in range(CHUNKS):
        v_copies[i].wait()
        below += tmm(q_ref[1, block(p, i)], q_ref[0, block(p, i)])
    cross[...] = below
    gpart[width:] = cross[pl.ds(pl.multiple_of(v * half, half), half)]

    def part_of(o):
        return pl.ds(pl.multiple_of(o * piece, piece), piece)

    def reduce_copy(k):
        o = at(k)
        return copy(gpart.at[part_of(o)], gslot.at[k], r_send.at[k], r_recv.at[k], device(o))

    repeat(1, owners, lambda k: when_owner(at(k), lambda: reduce_copy(k).start()))

    def whole(q):
        return pl.ds(pl.multiple_of(q * share, share), share)

    q_copies = []
    for k in range(1, np_):
        mine = q_ref.at[v, whole(p)]
        q_copies.append(copy(mine, mine, q_send.at[k], q_recv.at[k], {"pole": pole(k)}))
        q_copies[-1].start()

    def collect():
        repeat(1, owners, lambda k: reduce_copy(k).wait_recv())
        gslot[0] = gpart[part_of(me)]
        total = gslot[0]
        for k in range(1, owners):
            total += gslot[k]
        g_ref[v, part_of(me)] = total

    when_owner(me, collect)

    def gather_copy(k):
        mine = g_ref.at[v, part_of(me)]
        return copy(mine, mine, a_send.at[k], a_recv.at[k], device(at(k)))

    def forward_copy(k):
        theirs = g_ref.at[v, part_of(at(owners - k))]
        return copy(theirs, theirs, f_send.at[k], f_recv.at[k], other)

    when_owner(me, lambda: repeat(1, owners, lambda k: gather_copy(k).start()))
    when_owner(me, lambda: forward_copy(0).start())

    def hand_on(k):
        def act():
            gather_copy(k).wait_recv()
            forward_copy(k).start()

        when_owner(at(owners - k), act)

    repeat(1, owners, hand_on)

    def share_copy(k):
        theirs = q_ref.at[0, whole(pole(np_ - k))]
        return copy(theirs, theirs, h_send.at[k], h_recv.at[k], other)

    for k in range(1, np_):
        q_copies[k - 1].wait_recv()
        pl.when(v == 0)(share_copy(k).start)
    repeat(0, owners, lambda k: when_owner(at(owners - k), forward_copy(k).wait))
    for k in range(1, np_):
        pl.when(v == 1)(share_copy(k).wait_recv)
        pl.when(v == 0)(share_copy(k).wait_send)
        q_copies[k - 1].wait_send()
    repeat(1, owners, lambda k: when_owner(at(k), reduce_copy(k).wait_send))
    when_owner(me, lambda: repeat(1, owners, lambda k: gather_copy(k).wait_send()))


def eliminate(w):
    n = w.shape[0]
    sub = lax.broadcasted_iota(jnp.int32, (8, n), 0)
    lane = lax.broadcasted_iota(jnp.int32, (8, n), 1)
    groups = n // 8
    ws = [w[8 * g : 8 * g + 8] for g in range(groups)]
    es = [(lane == sub + 8 * g).astype(F32) for g in range(groups)]
    upper, lower = [], []
    for b in range(groups):
        k = 8 * b
        pw, pe = ws[b], es[b]
        cols = [jnp.broadcast_to(pw[:, k + j : k + j + 1], (8, n)) for j in range(8)]
        far = [
            [jnp.broadcast_to(ws[g][:, k + j : k + j + 1], (8, n)) for j in range(8)]
            for g in range(b + 1, groups)
        ]
        uw, ue = jnp.zeros_like(pw), jnp.zeros_like(pe)
        for j in range(8):
            at = sub == j
            c = cols[j]
            pivot = c[j : j + 1]
            root = lax.rsqrt(pivot)
            inverse = 1.0 / pivot
            rw, re = pw[j : j + 1], pe[j : j + 1]
            uw = jnp.where(at, rw * root, uw)
            ue = jnp.where(at, re * root, ue)
            rw, re = rw * inverse, re * inverse
            pw = jnp.where(at, rw, pw - c * rw)
            pe = jnp.where(at, re, pe - c * re)
            for m in range(j + 1, 8):
                rc = cols[m][j : j + 1] * inverse
                cols[m] = jnp.where(at, rc, cols[m] - c * rc)
        upper.append(uw)
        lower.append(ue)
        for g in range(b + 1, groups):
            for j in range(8):
                c = far[g - b - 1][j]
                ws[g] = ws[g] - c * pw[j : j + 1]
                es[g] = es[g] - c * pe[j : j + 1]
    u = jnp.concatenate(upper, axis=0)
    l = jnp.concatenate(lower, axis=0)
    row = lax.broadcasted_iota(jnp.int32, (n, n), 0)
    col = lax.broadcasted_iota(jnp.int32, (n, n), 1)
    return jnp.where(row <= col, u, 0.0), jnp.where(row >= col, l, 0.0)


def solve_kernel(rows_total, q_ref, g_ref, basis_ref, factor_ref):
    v = lax.axis_index("vec")
    width = g_ref.shape[2]
    scale = 1.0 / rows_total
    u11, i11 = eliminate(g_ref[0, :width] * scale)
    low = jnp.concatenate([g_ref[0, width:], g_ref[1, width:]], axis=0) * scale
    u12 = times(i11, low)
    schur = g_ref[1, :width] * scale - tmm(u12, u12)
    u22, i22 = eliminate(schur)
    factor_ref[:width, :width] = u11.T
    factor_ref[:width, width:] = jnp.zeros((width, width), F32)
    factor_ref[width:, :width] = u12.T
    factor_ref[width:, width:] = u22.T

    @pl.when(v == 0)
    def _():
        basis_ref[...] = times(q_ref[0], i11).astype(BF16)

    @pl.when(v == 1)
    def _():
        i21 = -hmm(i22, tmm(u12, i11))
        basis_ref[...] = (times(q_ref[0], i21) + times(q_ref[1], i22)).astype(BF16)


def body(right_side, inverse, coupling, weights):
    rows, width = right_side.shape
    edge = coupling.shape[2]
    nd, np_ = lax.axis_size("dom"), lax.axis_size("pole")
    owners = nd * np_
    total = width + width // 2
    vmem = pl.BlockSpec(memory_space=pltpu.VMEM)
    hbm = pl.BlockSpec(memory_space=pltpu.HBM)
    dma = pltpu.SemaphoreType.DMA
    q, g = pl.pallas_call(
        functools.partial(filter_kernel, nd, np_),
        out_shape=(
            jax.ShapeDtypeStruct((2, rows, width), F32),
            jax.ShapeDtypeStruct((2, total, width), F32),
        ),
        in_specs=[hbm, hbm, hbm, hbm],
        out_specs=(vmem, vmem),
        scratch_shapes=[
            pltpu.VMEM((rows, width), BF16),
            pltpu.VMEM((2, rows, rows), BF16),
            pltpu.VMEM((2, edge, edge), BF16),
            pltpu.SMEM((1, 2), F32),
            dma((6,)),
            pltpu.VMEM((rows, 2 * width), F32),
            pltpu.VMEM((2, 2, edge, 2 * width), BF16),
            pltpu.VMEM((2, 2, edge, 2 * width), BF16),
            pltpu.VMEM((np_, rows // np_, width), BF16),
            pltpu.VMEM((np_, rows // np_, width), BF16),
            pltpu.VMEM((np_, rows // np_, width), BF16),
            pltpu.VMEM((np_, rows // np_, width), BF16),
            pltpu.VMEM((width, width), F32),
            pltpu.VMEM((total, width), F32),
            pltpu.VMEM((owners, piece_of(total, owners), width), F32),
            dma((2, 2)), dma((2, 2)),
            dma((np_,)), dma((np_,)),
            dma((CHUNKS, np_)), dma((CHUNKS, np_)),
            dma((CHUNKS,)), dma((CHUNKS,)),
            dma((np_,)), dma((np_,)),
            dma((np_,)), dma((np_,)),
            dma((owners,)), dma((owners,)),
            dma((owners,)), dma((owners,)),
            dma((owners,)), dma((owners,)),
        ],
        compiler_params=pltpu.CompilerParams(
            collective_id=0, has_side_effects=True, vmem_limit_bytes=40 * 2**20
        ),
        name="filter",
    )(right_side, inverse, coupling, weights)
    return pl.pallas_call(
        functools.partial(solve_kernel, rows * nd),
        out_shape=(
            jax.ShapeDtypeStruct((rows, width), BF16),
            jax.ShapeDtypeStruct((2 * width, 2 * width), F32),
        ),
        in_specs=[vmem, vmem],
        out_specs=(vmem, vmem),
        compiler_params=pltpu.CompilerParams(vmem_limit_bytes=40 * 2**20),
        name="solve",
    )(q, g)


def solution(mesh):
    return jax.shard_map(
        body,
        mesh=mesh,
        in_specs=(
            P(("groups", "dom"), "vec"),
            P("pole", None, ("groups", "dom"), None),
            P(("groups", "dom"), None, None, None),
            P("pole", None),
        ),
        out_specs=(P(("groups", "dom"), "vec"), P("groups", None)),
        check_vma=False,
    )
```

time: 50 us -> 49.3 us (0.986)
  Pallas kernels: 44.4 us -> 43.7 us
    pallas_call x1, Pallas kernels: 34 us -> 33.3 us  [body(): pl.pallas_call(functools.partial(filter_kernel, nd, np_), out_shape=(jax....]
where the time goes in v2:
time: 49.3 us; the launch traced here: 49.1 us
  Pallas kernels  43.7 us (89%)
  local copies, waits for them, and re-layouts  4.73 us (10%)
  between operations  0.65 us (1%)
    pallas_call x1, Pallas kernels, body(): pl.pallas_call(functools.partial(filter_kernel, nd, np_), out_shape=(jax....  33.3 us
    pallas_call x1, Pallas kernels, body(): pl.pallas_call(functools.partial(solve_kernel, rows * nd), out_shape=(jax...  10.4 us
    unnamed x8, local copies, waits for them, and re-layouts  4.73 us

profile of v2, /device:TPU:1, one launch (start us, length us, event | category | flops | bytes accessed | tf_op | source)
XLA Modules:
  0.0 49.1 jit_solution(10085938916504502698)
XLA Ops:
  0.6 0.0 copy-start
  0.6 2.2 %copy-done = bf16[1,2,1024,1024]{3,2,1,0:T(8,128)(2,1)S(1)} copy-done((bf16[1,2,1024,1024]{3,2,1,0:T(8,128)(2,1)S(1)}, bf16[1,2,1024,1024]{3,2,1,0:T(8,128)(2,1)}, u32[]{:S(2)}) %copy-start) | copy-done | bytes 4194328
  2.8 0.0 copy-start.1
  2.8 0.9 %copy-done.1 = bf16[1024,128]{1,0:T(8,128)(2,1)S(1)} copy-done((bf16[1024,128]{1,0:T(8,128)(2,1)S(1)}, bf16[1024,128]{1,0:T(8,128)(2,1)}, u32[]{:S(2)}) %copy-start.1) | copy-done | bytes 262168
  3.8 0.0 copy-start.2
  3.8 0.9 %copy-done.2 = bf16[1,2,256,256]{3,2,1,0:T(8,128)(2,1)S(1)} copy-done((bf16[1,2,256,256]{3,2,1,0:T(8,128)(2,1)S(1)}, bf16[1,2,256,256]{3,2,1,0:T(8,128)(2,1)}, u32[]{:S(2)}) %copy-start.2) | copy-done | bytes 262168
  4.7 0.0 copy-start.3
  4.7 0.7 %copy-done.3 = f32[1,2]{1,0:T(1,128)S(1)} copy-done((f32[1,2]{1,0:T(1,128)S(1)}, f32[1,2]{1,0:T(1,128)}, u32[]{:S(2)}) %copy-start.3) | copy-done | bytes 32
  5.4 33.3 %filter.1 = (f32[2,1024,128]{2,1,0:T(8,128)S(1)}, f32[2,192,128]{2,1,0:T(8,128)S(1)}) custom-call(bf16[1024,128]{1,0:T(8,128)(2,1)S(1)} %copy-done.1, bf16[1,2,1024,1024]{3,2,1,0:T(8,128)(2,1)S(1)} %copy-done, bf16[1,2,256,256]{3,2,1,0:T(8,128)(2,1)S(1)} %copy-done.2, f32[1,2]{1,0:T(1,128)S(1)} %copy-done.3), custom_call_target="tpu_custom_call" | custom-call | tf_op jit(solution)/shard_map/filter/pallas_call | solution.py:391
  38.7 10.4 %solve.1 = (bf16[1024,128]{1,0:T(8,128)(2,1)}, f32[256,256]{1,0:T(8,128)}) custom-call(f32[2,1024,128]{2,1,0:T(8,128)S(1)} %get-tuple-element.4.q_ref, f32[2,192,128]{2,1,0:T(8,128)S(1)} %get-tuple-element.5.g_ref), custom_call_target="tpu_custom_call" | custom-call | tf_op jit(solution)/shard_map/solve/pallas_call | solution.py:430
Async XLA Ops:
  0.6 2.2 %copy-start = (bf16[1,2,1024,1024]{3,2,1,0:T(8,128)(2,1)S(1)}, bf16[1,2,1024,1024]{3,2,1,0:T(8,128)(2,1)}, u32[]{:S(2)}) copy-start(bf16[1,2,1024,1024]{3,2,1,0:T(8,128)(2,1)} %inv_hbm.1) | copy-start | bytes 12582916
  2.8 0.9 %copy-start.1 = (bf16[1024,128]{1,0:T(8,128)(2,1)S(1)}, bf16[1024,128]{1,0:T(8,128)(2,1)}, u32[]{:S(2)}) copy-start(bf16[1024,128]{1,0:T(8,128)(2,1)} %x_hbm.1) | copy-start | bytes 786436
  3.8 0.9 %copy-start.2 = (bf16[1,2,256,256]{3,2,1,0:T(8,128)(2,1)S(1)}, bf16[1,2,256,256]{3,2,1,0:T(8,128)(2,1)}, u32[]{:S(2)}) copy-start(bf16[1,2,256,256]{3,2,1,0:T(8,128)(2,1)} %k_hbm.1) | copy-start | bytes 786436
  4.7 0.7 %copy-start.3 = (f32[1,2]{1,0:T(1,128)S(1)}, f32[1,2]{1,0:T(1,128)}, u32[]{:S(2)}) copy-start(f32[1,2]{1,0:T(1,128)} %w_hbm.1) | copy-start | bytes 28
